TPU v7x, 32 devices: a whole 2x2x4 slice. The times are simulated.
32 devices in a mesh: rep: 2 (over x), ctx: 8 (over z, y), tp: 2 (over core).
Axes of the slice: x: 2, y: 2, z: 4, core: 2. Of those that a mesh axis runs over, the one named last changes fastest.
Arguments:
- queries: bfloat16 [4096, 4096], P(('rep', 'ctx'), 'tp'), parts along dimension 0, may hold values from -8 to 8
- rotated_key_rows: bfloat16 [4096, 512], P(('rep', 'ctx'), 'tp'), parts along dimension 0, may hold values from -8 to 8
- ordered_value_rows: bfloat16 [4096, 512], P(('rep', 'ctx'), 'tp'), parts along dimension 0, may hold values from -6 to 6
- block_order: int32 [32], P('rep'), parts along dimension 0, may hold values from 0 to 15, each once
- live_blocks: int32 [32, 12], P('rep'), parts along dimension 0, may hold values from -1 to 15, as said below
Outputs:
- attended: bfloat16 [4096, 4096], P(('rep', 'ctx', 'tp')), parts along dimension 0
- log_norm: float32 [64, 2048], P(('rep', 'tp'), 'ctx'), parts along dimension 0
There are 2 independent parts, one for each index of `rep`. A program takes and returns all parts, laid end to end along the dimension named above; each array names one. Nothing has to cross between parts.
Inputs may be any that keep to these rules, and one draw needn't show every extreme that they name: `live_blocks`: row s names block s in its first slot, then distinct blocks before s, then -1 in every unused slot; row 15 fills all 12 slots.
All inputs are finite; a program needn't handle non-finite values.
Results may differ from a plain program's by a relative error of at most 0.008.
Values may be sent and summed in bfloat16 or wider, within the bound.
No kernel may reach another device: no remote copies, remote signals or barrier semaphores. Data moves between devices by JAX's collectives and lax.ppermute only.
A program may use at most 128 MiB of HBM per device.

v0:
```python
import functools

import jax
import jax.numpy as jnp
import numpy as np
from jax import lax
from jax.experimental import pallas as pl
from jax.experimental.pallas import tpu as pltpu
from jax.sharding import PartitionSpec as P

HEAD_SIZE = 128
BLOCK_TOKENS = 128
SCALE2 = float(HEAD_SIZE**-0.5 * np.log2(np.e))
LN2 = float(np.log(2.0))
FAR = 1e30
VMEM_BYTES = 24 * 2**20
FULL_VMEM = 64 * 2**20
COST = 1024
CHUNK = 3


def tile(i):
    return slice(i * BLOCK_TOKENS, (i + 1) * BLOCK_TOKENS)


def attend(shard, qb, place, gaps, diagonal, kv_local, groups, qt_ref, ml_ref, acc_ref, finish=None):
    blocks = len(gaps)
    first = diagonal is not None
    keys_ref, values_ref = shard
    keys = [keys_ref[:, tile(i)] for i in range(kv_local)]
    values = [
        jnp.concatenate([values_ref[tile(j), tile(i)] for j in range(blocks)], axis=1) for i in range(kv_local)
    ]
    if first:
        key_row = lax.broadcasted_iota(jnp.int32, (BLOCK_TOKENS, BLOCK_TOKENS), 0)
        query_col = lax.broadcasted_iota(jnp.int32, (BLOCK_TOKENS, BLOCK_TOKENS), 1)
        causal = key_row <= query_col
    heads = [i * groups + g for g in range(groups) for i in range(kv_local)]
    scores, weights, rescales, ends = {}, {}, {}, {}

    def score(h):
        scores[h] = jnp.dot(keys[h // groups], qt_ref[qb, :, tile(h)], preferred_element_type=jnp.float32)

    def soften(h):
        whole = scores.pop(h)
        parts = [whole[tile(j)] * SCALE2 for j in range(blocks)]
        if first:
            parts[diagonal] = jnp.where(causal, parts[diagonal], -FAR)
        peak = functools.reduce(
            jnp.maximum, [jnp.max(part, axis=0, keepdims=True) - gap for part, gap in zip(parts, gaps)]
        )
        if not first:
            old_peak = ml_ref[place, 0:1, tile(h)]
            peak = jnp.maximum(peak, old_peak)
        exps = [jnp.exp2(part - (peak + gap)) for part, gap in zip(parts, gaps)]
        total = functools.reduce(jnp.add, [jnp.sum(e, axis=0, keepdims=True) for e in exps])
        if not first:
            rescales[h] = jnp.exp2(old_peak - peak)
            total = total + ml_ref[place, 1:2, tile(h)] * rescales[h]
        if finish:
            ends[h] = peak, total
        else:
            ml_ref[place, 0:1, tile(h)] = peak
            ml_ref[place, 1:2, tile(h)] = total
        weights[h] = jnp.concatenate([e.astype(jnp.bfloat16) for e in exps], axis=0)

    def weigh(h):
        weighted = jnp.dot(values[h // groups], weights.pop(h), preferred_element_type=jnp.float32)
        if not first:
            weighted = weighted + acc_ref[place, :, tile(h)] * rescales.pop(h)
        if finish:
            finish(h, *ends.pop(h), weighted)
        else:
            acc_ref[place, :, tile(h)] = weighted

    for t in range(len(heads) + 2):
        if t < len(heads):
            score(heads[t])
        if 1 <= t <= len(heads):
            soften(heads[t - 1])
        if t >= 2:
            weigh(heads[t - 2])


def split_shards(pieces, refs):
    shards, refs = [], list(refs)
    for count in pieces:
        if count == 2:
            shards.append((refs.pop(0), refs.pop(0)))
        else:
            shards.append(halves(refs.pop(0)))
    return shards, refs


def halves(shard_ref):
    rows = shard_ref.shape[0] // 2
    return shard_ref.at[0:rows, :], shard_ref.at[rows : 2 * rows, :]


def attend_shards(masks, blocks, first, count, flags_ref, shards, **rest):
    me = lax.axis_index("ctx")
    total = flags_ref.shape[0] // blocks
    for m, shard in zip(masks, shards):

        def step(place, carry):
            qb = first + place
            mine = [flags_ref[qb * total + (me ^ m) * blocks + j] for j in range(blocks)]

            @pl.when(functools.reduce(jnp.bitwise_or, mine) != 0)
            def _():
                gaps = [jnp.where(flag != 0, 0.0, FAR) for flag in mine]
                attend(shard, qb, place, gaps, None, **rest)

            return carry

        if count == 1:
            step(0, 0)
        else:
            lax.fori_loop(0, count, step, 0)


def pack_kernel(blocks, k_hbm, v_hbm, order_hbm, live_hbm, shard_ref, values_ref, flags_ref, v_buf, order_ref, live_ref, place_ref, sems):
    rows, width = v_buf.shape
    total, slots = order_ref.shape[0], live_ref.shape[1]
    pairs = [(v_hbm, v_buf), (k_hbm, shard_ref.at[0:rows, :]), (order_hbm, order_ref), (live_hbm, live_ref)]
    copies = [pltpu.make_async_copy(source, target, sems.at[i]) for i, (source, target) in enumerate(pairs)]
    for copy in copies:
        copy.start()

    def clear(i, carry):
        flags_ref[i] = 0
        return carry

    def invert(b, carry):
        place_ref[order_ref[b]] = b
        return carry

    lax.fori_loop(0, blocks * total, clear, 0, unroll=8)
    copies[2].wait()
    lax.fori_loop(0, total, invert, 0, unroll=8)
    copies[3].wait()
    me = lax.axis_index("ctx")
    for qb in range(blocks):
        row = order_ref[me * blocks + qb]

        def mark(slot, carry):
            entry = live_ref[row, slot]
            spot = qb * total + place_ref[jnp.maximum(entry, 0)]
            flags_ref[jnp.where(entry >= 0, spot, blocks * total)] = 1
            return carry

        lax.fori_loop(0, slots, mark, 0, unroll=4)
    copies[0].wait()
    for j in range(rows // BLOCK_TOKENS):
        for i in range(width // HEAD_SIZE):
            turned = v_buf[tile(j), tile(i)].T
            shard_ref[tile(rows // BLOCK_TOKENS + j), tile(i)] = turned
            values_ref[tile(j), tile(i)] = turned
    copies[1].wait()


def tick_kernel(_shard, tick_ref):
    tick_ref[0] = 0


def own_kernel(blocks, kv_local, groups, flags_ref, q_ref, own_ref, qt_ref, ml_ref, acc_ref):
    me = lax.axis_index("ctx")
    total = flags_ref.shape[0] // blocks
    for qb in range(blocks):
        for h in range(kv_local * groups):
            qt_ref[qb, :, tile(h)] = q_ref[tile(qb), tile(h)].T
        flags = [flags_ref[qb * total + me * blocks + j] for j in range(blocks)]
        gaps = [0.0 if j == qb else jnp.where(flags[j] != 0, 0.0, FAR) for j in range(blocks)]
        attend(halves(own_ref), qb, qb, gaps, qb, kv_local, groups, qt_ref, ml_ref, acc_ref)


def more_kernel(masks, pieces, blocks, kv_local, groups, flags_ref, qt_ref, ml_in, acc_in, *refs):
    shards, (ml_ref, acc_ref) = split_shards(pieces, refs)
    ml_ref[...] = ml_in[...]
    acc_ref[...] = acc_in[...]
    attend_shards(
        masks, blocks, 0, blocks, flags_ref, shards,
        kv_local=kv_local, groups=groups, qt_ref=qt_ref, ml_ref=ml_ref, acc_ref=acc_ref,
    )


def last_kernel(masks, pieces, blocks, part, step, cores, kv_local, groups, flags_ref, qt_ref, ml_in, acc_in, *refs):
    shards, (out_ref, norm_ref, ml_ref, acc_ref) = split_shards(pieces, refs)
    to = lax.rem(lax.axis_index("tp") + step, cores)
    for j in range(part):
        ml_ref[j] = ml_in[to * part + j]
        acc_ref[j] = acc_in[to * part + j]
    rest = dict(kv_local=kv_local, groups=groups, qt_ref=qt_ref, ml_ref=ml_ref, acc_ref=acc_ref)
    attend_shards(masks[:-1], blocks, to * part, part, flags_ref, shards[:-1], **rest)
    me = lax.axis_index("ctx")
    total = flags_ref.shape[0] // blocks
    for j in range(part):

        def finish(h, peak, denominator, weighted):
            normed = weighted * (1.0 / denominator)
            out_ref[tile(j), tile(h)] = normed.astype(jnp.bfloat16).T
            norm_ref[h : h + 1, tile(j)] = peak * LN2 + jnp.log(denominator)

        qb = to * part + j
        mine = [flags_ref[qb * total + (me ^ masks[-1]) * blocks + b] for b in range(blocks)]
        some = functools.reduce(jnp.bitwise_or, mine)

        @pl.when(some != 0)
        def _():
            gaps = [jnp.where(flag != 0, 0.0, FAR) for flag in mine]
            attend(shards[-1], qb, j, gaps, None, finish=finish, **rest)

        @pl.when(some == 0)
        def _():
            for h in range(kv_local * groups):
                finish(h, ml_ref[j, 0:1, tile(h)], ml_ref[j, 1:2, tile(h)], acc_ref[j, :, tile(h)])


def place_kernel(cores, *refs):
    outs, norms, (out_hbm, norm_hbm, sems) = refs[:cores], refs[cores : 2 * cores], refs[2 * cores :]
    core = lax.axis_index("tp")
    copies = []
    for step in range(cores):
        origin = lax.rem(core + cores - step, cores)
        width = outs[step].shape[1]
        columns = pl.ds(pl.multiple_of(origin * width, HEAD_SIZE), width)
        copies.append(pltpu.make_async_copy(outs[step], out_hbm.at[:, columns], sems.at[step]))
    for step in range(cores):
        to = lax.rem(core + step, cores)
        width = norms[step].shape[1]
        columns = pl.ds(pl.multiple_of(to * width, BLOCK_TOKENS), width)
        copies.append(pltpu.make_async_copy(norms[step], norm_hbm.at[:, columns], sems.at[cores + step]))
    for copy in copies:
        copy.start()
    for copy in copies:
        copy.wait()


def body(queries, key_rows, value_rows, block_order, live_blocks):
    rows, width = queries.shape
    kv_local = key_rows.shape[1] // HEAD_SIZE
    heads = width // HEAD_SIZE
    groups = heads // kv_local
    blocks = rows // BLOCK_TOKENS
    shards = lax.axis_size("ctx")
    cores = lax.axis_size("tp")
    part = blocks // cores

    vmem = pl.BlockSpec(memory_space=pltpu.VMEM)
    smem = pl.BlockSpec(memory_space=pltpu.SMEM)
    hbm = pl.BlockSpec(memory_space=pltpu.HBM)
    qt_shape = jax.ShapeDtypeStruct((blocks, HEAD_SIZE, width), jnp.bfloat16)
    ml_shape = jax.ShapeDtypeStruct((blocks, 2, width), jnp.float32)
    acc_shape = jax.ShapeDtypeStruct((blocks, HEAD_SIZE, width), jnp.float32)

    def call(kernel, name, limit=VMEM_BYTES, **options):
        return pl.pallas_call(
            kernel,
            name=name,
            compiler_params=pltpu.CompilerParams(vmem_limit_bytes=limit),
            cost_estimate=pl.CostEstimate(flops=COST, bytes_accessed=COST, transcendentals=0),
            **options,
        )

    def swap(array, distance):
        return lax.ppermute(array, "ctx", [(i, i ^ distance) for i in range(shards)])

    bits = [1 << i for i in range(shards.bit_length() - 1)]
    top = bits[-1]
    shard, values, flags = call(
        functools.partial(pack_kernel, blocks),
        "pack",
        FULL_VMEM,
        in_specs=[hbm] * 4,
        out_specs=[vmem, vmem, smem],
        out_shape=[
            jax.ShapeDtypeStruct((2 * rows, kv_local * HEAD_SIZE), jnp.bfloat16),
            jax.ShapeDtypeStruct((rows, kv_local * HEAD_SIZE), jnp.bfloat16),
            jax.ShapeDtypeStruct((blocks * block_order.shape[0] + 1,), jnp.int32),
        ],
        scratch_shapes=[
            pltpu.VMEM(value_rows.shape, jnp.bfloat16),
            pltpu.SMEM(block_order.shape, jnp.int32),
            pltpu.SMEM(live_blocks.shape, jnp.int32),
            pltpu.SMEM(block_order.shape, jnp.int32),
            pltpu.SemaphoreType.DMA((4,)),
        ],
    )(key_rows, value_rows, block_order, live_blocks)
    got = {top: [swap(shard, top)]}
    for bit in reversed(bits[1:-1]):
        got[bit] = [swap(shard, bit)]
    got[1] = [swap(key_rows, 1), swap(values, 1)]

    qt, ml, acc = call(
        functools.partial(own_kernel, blocks, kv_local, groups),
        "own_shard",
        in_specs=[smem] + [vmem] * 2,
        out_specs=[vmem] * 3,
        out_shape=[qt_shape, ml_shape, acc_shape],
    )(flags, queries, shard)

    def more(masks, ml, acc):
        return call(
            functools.partial(more_kernel, masks, [len(got[m]) for m in masks], blocks, kv_local, groups),
            "more_shards",
            in_specs=[smem] + [vmem] * (3 + sum(len(got[m]) for m in masks)),
            out_specs=[vmem] * 2,
            out_shape=[ml_shape, acc_shape],
        )(flags, qt, ml, acc, *[array for m in masks for array in got[m]])

    def last(masks, step, ml, acc):
        arrays = [array for m in masks for array in got[m]]
        return call(
            functools.partial(
                last_kernel, masks, [len(got[m]) for m in masks], blocks, part, step, cores, kv_local, groups
            ),
            "last_shards",
            in_specs=[smem] + [vmem] * (3 + len(arrays)),
            out_specs=[vmem, vmem],
            out_shape=[
                jax.ShapeDtypeStruct((part * BLOCK_TOKENS, width), jnp.bfloat16),
                jax.ShapeDtypeStruct((heads, part * BLOCK_TOKENS), jnp.float32),
            ],
            scratch_shapes=[
                pltpu.VMEM((part, *ml_shape.shape[1:]), jnp.float32),
                pltpu.VMEM((part, *acc_shape.shape[1:]), jnp.float32),
            ],
        )(flags, qt, ml, acc, *arrays)

    def after(arrays, *others):
        return [lax.optimization_barrier((array,) + others)[0] for array in arrays]

    several = sorted((m for m in range(shards) if m.bit_count() > 1), key=lambda m: (m.bit_count(), m))
    ml, acc = more([1], ml, acc)
    got[top] = after(got[top], acc)
    for bit in reversed(bits[1:-1]):
        got[bit] = after(got[bit], got[top][0])
        got[top] = after(got[top], got[bit][0])
    for m in several:
        if m & top and m.bit_count() == 2:
            got[m] = [swap(array, m & -m) for array in got[m & (m - 1)]]
    ml, acc = more(bits[1:], ml, acc)
    got[3] = [swap(jnp.concatenate(after(got[1], acc), axis=0), 2)]
    for m in several:
        if m not in got:
            got[m] = [swap(array, m & -m) for array in after(got[m & (m - 1)], acc)]
    final = [3, several[-1]]
    ready = [m for m in several if m not in final]
    for i in range(0, len(ready), CHUNK):
        ml, acc = more(ready[i : i + CHUNK], ml, acc)

    outs, norms = [None] * cores, [None] * cores
    for step in range(cores - 1, -1, -1):
        outs[step], norms[step] = last(final, step, ml, acc)
        if step:
            outs[step] = lax.ppermute(outs[step], "tp", [(i, (i + step) % cores) for i in range(cores)])
    return call(
        functools.partial(place_kernel, cores),
        "place",
        in_specs=[vmem] * (2 * cores),
        out_specs=[hbm, hbm],
        out_shape=[
            jax.ShapeDtypeStruct((part * BLOCK_TOKENS, cores * width), jnp.bfloat16),
            jax.ShapeDtypeStruct((heads, rows), jnp.float32),
        ],
        scratch_shapes=[pltpu.SemaphoreType.DMA((2 * cores,))],
    )(*outs, *norms)


def solution(mesh):
    placed = (
        P(("rep", "ctx"), "tp"),
        P(("rep", "ctx"), "tp"),
        P(("rep", "ctx"), "tp"),
        P("rep"),
        P("rep", None),
    )
    return jax.shard_map(
        body,
        mesh=mesh,
        in_specs=placed,
        out_specs=(P(("rep", "ctx", "tp"), None), P(("rep", "tp"), "ctx")),
        check_vma=False,
    )
```

profile of v0, /device:TPU:29, one launch (start us, length us, event | category | flops | bytes accessed | tf_op | source)
XLA Modules:
  0.0 40.1 jit_solution(5633305009257597015)
XLA Ops:
  0.6 1.9 %pack.1 = (bf16[512,256]{1,0:T(8,128)(2,1)}, bf16[256,256]{1,0:T(8,128)(2,1)}, s32[33]{0:T(128)}) custom-call(bf16[256,256]{1,0:T(8,128)(2,1)} %k_hbm.1, bf16[256,256]{1,0:T(8,128)(2,1)} %v_hbm.1, s32[16]{0:T(128)} %order_hbm.1, s32[16,12]{1,0:T(8,128)} %live_hbm.1), custom_call_target="tpu_custom_call" | custom-call | flops 1024 | bytes 1024 | tf_op jit(solution)/shard_map/pack/pallas_call | solution.py:270
  2.6 0.1 collective-permute-start.3
  2.7 0.2 collective-permute-start.2
  2.9 0.2 collective-permute-start
  3.1 1.2 %collective-permute-start.1 = (bf16[256,256]{1,0:T(8,128)(2,1)}, bf16[256,256]{1,0:T(8,128)(2,1)S(1)}, u32[]{:S(2)}, u32[]{:S(2)}) collective-permute-start(bf16[256,256]{1,0:T(8,128)(2,1)} %get-tuple-element.29), channel_id=1, source_target_pairs={{0,2},{2,0},{4,6},{6,4},{8,10},{10,8},{12,14},{14,12},{1,3},{3,1},... | collective-permute-start | bytes 393224 | tf_op jit(solution)/shard_map/ppermute | solution.py:266
  4.4 0.0 copy-start
  4.4 1.2 %copy-done = bf16[256,2048]{1,0:T(8,128)(2,1)S(1)} copy-done((bf16[256,2048]{1,0:T(8,128)(2,1)S(1)}, bf16[256,2048]{1,0:T(8,128)(2,1)}, u32[]{:S(2)}) %copy-start) | copy-done | bytes 1048600
  5.6 0.0 copy-start.1
  5.6 0.9 %copy-done.1 = bf16[512,256]{1,0:T(8,128)(2,1)S(1)} copy-done((bf16[512,256]{1,0:T(8,128)(2,1)S(1)}, bf16[512,256]{1,0:T(8,128)(2,1)}, u32[]{:S(2)}) %copy-start.1) | copy-done | bytes 262168
  6.5 0.0 copy-start.2
  6.5 0.7 %copy-done.2 = s32[33]{0:T(128)S(1)} copy-done((s32[33]{0:T(128)S(1)}, s32[33]{0:T(128)}, u32[]{:S(2)}) %copy-start.2) | copy-done | bytes 156
  7.2 2.4 %own_shard.1 = (bf16[2,128,2048]{2,1,0:T(8,128)(2,1)S(1)}, f32[2,2,2048]{2,1,0:T(2,128)S(1)}, f32[2,128,2048]{2,1,0:T(8,128)S(1)}) custom-call(s32[33]{0:T(128)S(1)} %copy-done.2, bf16[256,2048]{1,0:T(8,128)(2,1)S(1)} %copy-done, bf16[512,256]{1,0:T(8,128)(2,1)S(1)} %copy-done.1), custom_call_target="tpu_custom_call" | custom-call | flops 1024 | bytes 1024 | tf_op jit(solution)/shard_map/own_shard/pallas_call | solution.py:294
  9.6 0.0 collective-permute-done.refs_0_
  9.6 0.1 collective-permute-done.1.refs_1_
  9.7 2.6 %more_shards.3 = (f32[2,2,2048]{2,1,0:T(2,128)S(1)}, f32[2,128,2048]{2,1,0:T(8,128)S(1)}) custom-call(s32[33]{0:T(128)S(1)} %copy-done.2, bf16[2,128,2048]{2,1,0:T(8,128)(2,1)S(1)} %get-tuple-element.26.qt_ref, f32[2,2,2048]{2,1,0:T(2,128)S(1)} %get-tuple-element.27.ml_in, f32[2,128,2048]{2,1,0:T(8,128)S(1)} %get-tuple-element.28.acc_in, ...), custom_call_target="tpu_custom_call" | custom-call | flops 1024 | bytes 1024 | tf_op jit(solution)/shard_map/more_shards/pallas_call | solution.py:303
  12.4 5.1 %collective-permute-done.3.refs_1_ = bf16[512,256]{1,0:T(8,128)(2,1)S(1)} collective-permute-done((bf16[512,256]{1,0:T(8,128)(2,1)}, bf16[512,256]{1,0:T(8,128)(2,1)S(1)}, u32[]{:S(2)}, u32[]{:S(2)}) %collective-permute-start.3) | collective-permute-done | bytes 262176 | tf_op jit(solution)/shard_map/ppermute | solution.py:266
  17.5 0.0 collective-permute-done.2.refs_0_
  17.5 0.0 collective-permute-start.5
  17.5 0.2 collective-permute-start.4
  17.7 0.0 copy-start.3
  17.7 4.6 %more_shards.4 = (f32[2,2,2048]{2,1,0:T(2,128)S(1)}, f32[2,128,2048]{2,1,0:T(8,128)S(1)}) custom-call(s32[33]{0:T(128)S(1)} %copy-done.2, bf16[2,128,2048]{2,1,0:T(8,128)(2,1)S(1)} %get-tuple-element.26.qt_ref, f32[2,2,2048]{2,1,0:T(2,128)S(1)} %get-tuple-element.30.ml_in, f32[2,128,2048]{2,1,0:T(8,128)S(1)} %get-tuple-element.31.acc_in, ...), custom_call_target="tpu_custom_call" | custom-call | flops 1024 | bytes 1024 | tf_op jit(solution)/shard_map/more_shards/pallas_call | solution.py:303
  22.4 0.1 collective-permute-start.6
  22.5 2.4 %collective-permute-done.5.refs_1_ = bf16[512,256]{1,0:T(8,128)(2,1)S(1)} collective-permute-done((bf16[512,256]{1,0:T(8,128)(2,1)S(1)}, bf16[512,256]{1,0:T(8,128)(2,1)S(1)}, u32[]{:S(2)}, u32[]{:S(2)}) %collective-permute-start.5) | collective-permute-done | bytes 262176 | tf_op jit(solution)/shard_map/ppermute | solution.py:266
  24.9 0.2 collective-permute-start.7
  25.1 0.0 collective-permute-done.4.refs_0_
  25.1 0.0 copy-done.3
  25.1 3.7 %more_shards.5 = (f32[2,2,2048]{2,1,0:T(2,128)S(1)}, f32[2,128,2048]{2,1,0:T(8,128)S(1)}) custom-call(s32[33]{0:T(128)S(1)} %copy-done.3, bf16[2,128,2048]{2,1,0:T(8,128)(2,1)S(1)} %get-tuple-element.26.qt_ref, f32[2,2,2048]{2,1,0:T(2,128)S(1)} %get-tuple-element.35.ml_in, f32[2,128,2048]{2,1,0:T(8,128)S(1)} %get-tuple-element.36.acc_in, ...), custom_call_target="tpu_custom_call" | custom-call | flops 1024 | bytes 1024 | tf_op jit(solution)/shard_map/more_shards/pallas_call | solution.py:303
  28.8 2.1 %collective-permute-done.6.refs_0_ = bf16[512,256]{1,0:T(8,128)(2,1)S(1)} collective-permute-done((bf16[512,256]{1,0:T(8,128)(2,1)S(1)}, bf16[512,256]{1,0:T(8,128)(2,1)S(1)}, u32[]{:S(2)}, u32[]{:S(2)}) %collective-permute-start.6) | collective-permute-done | bytes 262176 | tf_op jit(solution)/shard_map/ppermute | solution.py:266
  30.8 0.0 collective-permute-done.7.refs_1_
  30.8 2.7 %last_shards.3 = (bf16[128,2048]{1,0:T(8,128)(2,1)S(1)}, f32[16,128]{1,0:T(8,128)S(1)}) custom-call(s32[33]{0:T(128)S(1)} %copy-done.3, bf16[2,128,2048]{2,1,0:T(8,128)(2,1)S(1)} %get-tuple-element.26.qt_ref, f32[2,2,2048]{2,1,0:T(2,128)S(1)} %get-tuple-element.37.ml_in, f32[2,128,2048]{2,1,0:T(8,128)S(1)} %get-tuple-element.38.acc_in, ...), custom_call_target="tpu_custom_call" | custom-call | flops 1024 | bytes 1024 | tf_op jit(solution)/shard_map/last_shards/pallas_call | solution.py:313
  33.5 2.8 %collective-permute-start.8 = (bf16[128,2048]{1,0:T(8,128)(2,1)S(1)}, bf16[128,2048]{1,0:T(8,128)(2,1)S(1)}, u32[]{:S(2)}, u32[]{:S(2)}) collective-permute-start(bf16[128,2048]{1,0:T(8,128)(2,1)S(1)} %get-tuple-element.43), channel_id=1, source_target_pairs={{0,1},{1,0},{2,3},{3,2},{4,5},{5,4},{6,7},{7,6},{8,9},{9,8},{10,11... | collective-permute-start | bytes 1572872 | tf_op jit(solution)/shard_map/ppermute | solution.py:356
  36.4 2.7 %last_shards.2 = (bf16[128,2048]{1,0:T(8,128)(2,1)S(1)}, f32[16,128]{1,0:T(8,128)S(1)}) custom-call(s32[33]{0:T(128)S(1)} %copy-done.3, bf16[2,128,2048]{2,1,0:T(8,128)(2,1)S(1)} %get-tuple-element.26.qt_ref, f32[2,2,2048]{2,1,0:T(2,128)S(1)} %get-tuple-element.37.ml_in, f32[2,128,2048]{2,1,0:T(8,128)S(1)} %get-tuple-element.38.acc_in, ...), custom_call_target="tpu_custom_call" | custom-call | flops 1024 | bytes 1024 | tf_op jit(solution)/shard_map/last_shards/pallas_call | solution.py:313
  39.1 0.0 collective-permute-done.8.refs_1_
  39.1 1.0 %place.1 = (bf16[128,4096]{1,0:T(8,128)(2,1)}, f32[16,256]{1,0:T(8,128)}) custom-call(bf16[128,2048]{1,0:T(8,128)(2,1)S(1)} %get-tuple-element.42.refs_0_, bf16[128,2048]{1,0:T(8,128)(2,1)S(1)} %collective-permute-done.8.refs_1_, f32[16,128]{1,0:T(8,128)S(1)} %get-tuple-element.44.refs_2_, f32[16,128]{1,0:T(8,128)S(1)} %get-tuple-element.45.refs_3_), custom_call_target="tpu_custom_call" | custom-call | flops 1024 | bytes 1024 | tf_op jit(solution)/shard_map/place/pallas_call | solution.py:357
  (1 shorter events, 0.0 us)
Async XLA Ops:
  2.6 14.9 %collective-permute-start.3 = (bf16[512,256]{1,0:T(8,128)(2,1)}, bf16[512,256]{1,0:T(8,128)(2,1)S(1)}, u32[]{:S(2)}, u32[]{:S(2)}) collective-permute-start(bf16[512,256]{1,0:T(8,128)(2,1)} %get-tuple-element.25.own_ref), channel_id=1, source_target_pairs={{0,8},{2,10},{4,12},{6,14},{8,0},{10,2},{12,4},{14,6},{1,9},{3,11}... | collective-permute-start | bytes 786440 | tf_op jit(solution)/shard_map/ppermute | solution.py:266
  2.7 14.8 %collective-permute-start.2 = (bf16[512,256]{1,0:T(8,128)(2,1)}, bf16[512,256]{1,0:T(8,128)(2,1)S(1)}, u32[]{:S(2)}, u32[]{:S(2)}) collective-permute-start(bf16[512,256]{1,0:T(8,128)(2,1)} %get-tuple-element.25.own_ref), channel_id=1, source_target_pairs={{0,4},{2,6},{4,0},{6,2},{8,12},{10,14},{12,8},{14,10},{1,5},{3,7},... | collective-permute-start | bytes 786440 | tf_op jit(solution)/shard_map/ppermute | solution.py:266
  2.9 6.7 %collective-permute-start = (bf16[256,256]{1,0:T(8,128)(2,1)}, bf16[256,256]{1,0:T(8,128)(2,1)S(1)}, u32[]{:S(2)}, u32[]{:S(2)}) collective-permute-start(bf16[256,256]{1,0:T(8,128)(2,1)} %k_hbm.1), channel_id=1, source_target_pairs={{0,2},{2,0},{4,6},{6,4},{8,10},{10,8},{12,14},{14,12},{1,3},{3,1},... | collective-permute-start | bytes 393224 | tf_op jit(solution)/shard_map/ppermute | solution.py:266
  3.1 6.6 %collective-permute-start.1 = (bf16[256,256]{1,0:T(8,128)(2,1)}, bf16[256,256]{1,0:T(8,128)(2,1)S(1)}, u32[]{:S(2)}, u32[]{:S(2)}) collective-permute-start(bf16[256,256]{1,0:T(8,128)(2,1)} %get-tuple-element.29), channel_id=1, source_target_pairs={{0,2},{2,0},{4,6},{6,4},{8,10},{10,8},{12,14},{14,12},{1,3},{3,1},... | collective-permute-start | bytes 393224 | tf_op jit(solution)/shard_map/ppermute | solution.py:266
  4.4 1.2 %copy-start = (bf16[256,2048]{1,0:T(8,128)(2,1)S(1)}, bf16[256,2048]{1,0:T(8,128)(2,1)}, u32[]{:S(2)}) copy-start(bf16[256,2048]{1,0:T(8,128)(2,1)} %q_ref.1) | copy-start | bytes 3145732
  5.6 0.9 %copy-start.1 = (bf16[512,256]{1,0:T(8,128)(2,1)S(1)}, bf16[512,256]{1,0:T(8,128)(2,1)}, u32[]{:S(2)}) copy-start(bf16[512,256]{1,0:T(8,128)(2,1)} %get-tuple-element.25.own_ref) | copy-start | bytes 786436
  6.5 0.7 %copy-start.2 = (s32[33]{0:T(128)S(1)}, s32[33]{0:T(128)}, u32[]{:S(2)}) copy-start(s32[33]{0:T(128)} %get-tuple-element.24.flags_ref) | copy-start | bytes 400
  17.5 7.4 %collective-permute-start.5 = (bf16[512,256]{1,0:T(8,128)(2,1)S(1)}, bf16[512,256]{1,0:T(8,128)(2,1)S(1)}, u32[]{:S(2)}, u32[]{:S(2)}) collective-permute-start(bf16[512,256]{1,0:T(8,128)(2,1)S(1)} %collective-permute-done.3.refs_1_), channel_id=1, source_target_pairs={{0,4},{2,6},{4,0},{6,2},{8,12},{10,14},{12,8},{14,10},{1,5},{3,7},... | collective-permute-start | bytes 786440 | tf_op jit(solution)/shard_map/ppermute | solution.py:266
  17.5 7.6 %collective-permute-start.4 = (bf16[512,256]{1,0:T(8,128)(2,1)S(1)}, bf16[512,256]{1,0:T(8,128)(2,1)S(1)}, u32[]{:S(2)}, u32[]{:S(2)}) collective-permute-start(bf16[512,256]{1,0:T(8,128)(2,1)S(1)} %collective-permute-done.3.refs_1_), channel_id=1, source_target_pairs={{0,2},{2,0},{4,6},{6,4},{8,10},{10,8},{12,14},{14,12},{1,3},{3,1},... | collective-permute-start | bytes 786440 | tf_op jit(solution)/shard_map/ppermute | solution.py:266
  17.7 7.4 %copy-start.3 = (s32[33]{0:T(128)S(1)}, s32[33]{0:T(128)}, u32[]{:S(2)}) copy-start(s32[33]{0:T(128)} %get-tuple-element.24.flags_ref) | copy-start | bytes 400
  22.4 8.5 %collective-permute-start.6 = (bf16[512,256]{1,0:T(8,128)(2,1)S(1)}, bf16[512,256]{1,0:T(8,128)(2,1)S(1)}, u32[]{:S(2)}, u32[]{:S(2)}) collective-permute-start(bf16[512,256]{1,0:T(8,128)(2,1)S(1)} %pad_maximum_fusion), channel_id=1, source_target_pairs={{0,4},{2,6},{4,0},{6,2},{8,12},{10,14},{12,8},{14,10},{1,5},{3,7},... | collective-permute-start | bytes 786440 | tf_op jit(solution)/shard_map/ppermute | solution.py:266
  24.9 6.0 %collective-permute-start.7 = (bf16[512,256]{1,0:T(8,128)(2,1)S(1)}, bf16[512,256]{1,0:T(8,128)(2,1)S(1)}, u32[]{:S(2)}, u32[]{:S(2)}) collective-permute-start(bf16[512,256]{1,0:T(8,128)(2,1)S(1)} %collective-permute-done.5.refs_1_), channel_id=1, source_target_pairs={{0,2},{2,0},{4,6},{6,4},{8,10},{10,8},{12,14},{14,12},{1,3},{3,1},... | collective-permute-start | bytes 786440 | tf_op jit(solution)/shard_map/ppermute | solution.py:266
  33.5 5.5 %collective-permute-start.8 = (bf16[128,2048]{1,0:T(8,128)(2,1)S(1)}, bf16[128,2048]{1,0:T(8,128)(2,1)S(1)}, u32[]{:S(2)}, u32[]{:S(2)}) collective-permute-start(bf16[128,2048]{1,0:T(8,128)(2,1)S(1)} %get-tuple-element.43), channel_id=1, source_target_pairs={{0,1},{1,0},{2,3},{3,2},{4,5},{5,4},{6,7},{7,6},{8,9},{9,8},{10,11... | collective-permute-start | bytes 1572872 | tf_op jit(solution)/shard_map/ppermute | solution.py:356
where the time goes:
time: 40.4 us; the launch traced here: 40.1 us
  Pallas kernels  21.7 us (54%)
  waiting for transfers between devices  9.7 us (24%)
  starting transfers between devices  5.13 us (13%)
  local copies, waits for them, and re-layouts  2.83 us (7%)
  between operations  0.73 us (2%)
    pallas_call x3, Pallas kernels, more(): call(functools.partial(more_kernel, masks, [len(got[m]) for m in masks],...  10.9 us
    ppermute x8, waiting for transfers between devices, swap(): lax.ppermute(array, 'ctx', [(i, i ^ distance) for i in range(shards)])  9.7 us
    pallas_call x2, Pallas kernels, last(): call(functools.partial(last_kernel, masks, [len(got[m]) for m in masks],...  5.38 us
    unnamed x8, local copies, waits for them, and re-layouts  2.83 us
    ppermute x1, starting transfers between devices, body(): lax.ppermute(outs[step], 'tp', [(i, (i + step) % cores) for i in range(co...  2.82 us
    pallas_call x1, Pallas kernels, body(): call(functools.partial(own_kernel, blocks, kv_local, groups), 'own_shard'...  2.41 us
    ppermute x8, starting transfers between devices, swap(): lax.ppermute(array, 'ctx', [(i, i ^ distance) for i in range(shards)])  2.31 us
    pallas_call x1, Pallas kernels, body(): call(functools.partial(pack_kernel, blocks), 'pack', FULL_VMEM, in_specs=...  1.95 us
  transfers between devices with their start and end apart: 9, of which 4 were waited for; matrix products, arithmetic and copies ran while one was open for 0% of the time, Pallas kernels for 40%

commit v1 on v0

--- a/solution.py
+++ b/solution.py
@@ -14,7 +14,6 @@
 LN2 = float(np.log(2.0))
 FAR = 1e30
 VMEM_BYTES = 24 * 2**20
-FULL_VMEM = 64 * 2**20
 COST = 1024
 CHUNK = 3
 
@@ -97,18 +96,22 @@
     return shard_ref.at[0:rows, :], shard_ref.at[rows : 2 * rows, :]
 
 
-def attend_shards(masks, blocks, first, count, flags_ref, shards, **rest):
-    me = lax.axis_index("ctx")
-    total = flags_ref.shape[0] // blocks
+def gap_rows(gaps_ref, blocks, qb, mask):
+    total = gaps_ref.shape[0] // blocks
+    first = qb * total + (lax.axis_index("ctx") ^ mask) * blocks
+    gaps = [gaps_ref[first + j] for j in range(blocks)]
+    return gaps, functools.reduce(jnp.minimum, gaps)[0, 0] < FAR
+
+
+def attend_shards(masks, blocks, first, count, gaps_ref, shards, **rest):
     for m, shard in zip(masks, shards):
 
         def step(place, carry):
             qb = first + place
-            mine = [flags_ref[qb * total + (me ^ m) * blocks + j] for j in range(blocks)]
-
-            @pl.when(functools.reduce(jnp.bitwise_or, mine) != 0)
+            gaps, some = gap_rows(gaps_ref, blocks, qb, m)
+
+            @pl.when(some)
             def _():
-                gaps = [jnp.where(flag != 0, 0.0, FAR) for flag in mine]
                 attend(shard, qb, place, gaps, None, **rest)
 
             return carry
@@ -119,10 +122,24 @@
             lax.fori_loop(0, count, step, 0)
 
 
-def pack_kernel(blocks, k_hbm, v_hbm, order_hbm, live_hbm, shard_ref, values_ref, flags_ref, v_buf, order_ref, live_ref, place_ref, sems):
+def pack_kernel(k_hbm, v_hbm, shard_ref, values_ref, v_buf, sems):
     rows, width = v_buf.shape
+    values = pltpu.make_async_copy(v_hbm, v_buf, sems.at[0])
+    keys = pltpu.make_async_copy(k_hbm, shard_ref.at[0:rows, :], sems.at[1])
+    values.start()
+    keys.start()
+    values.wait()
+    for j in range(rows // BLOCK_TOKENS):
+        for i in range(width // HEAD_SIZE):
+            turned = v_buf[tile(j), tile(i)].T
+            shard_ref[tile(rows // BLOCK_TOKENS + j), tile(i)] = turned
+            values_ref[tile(j), tile(i)] = turned
+    keys.wait()
+
+
+def gaps_kernel(blocks, order_hbm, live_hbm, gaps_ref, flags_ref, order_ref, live_ref, place_ref, sems):
     total, slots = order_ref.shape[0], live_ref.shape[1]
-    pairs = [(v_hbm, v_buf), (k_hbm, shard_ref.at[0:rows, :]), (order_hbm, order_ref), (live_hbm, live_ref)]
+    pairs = [(order_hbm, order_ref), (live_hbm, live_ref)]
     copies = [pltpu.make_async_copy(source, target, sems.at[i]) for i, (source, target) in enumerate(pairs)]
     for copy in copies:
         copy.start()
@@ -136,9 +153,9 @@
         return carry
 
     lax.fori_loop(0, blocks * total, clear, 0, unroll=8)
-    copies[2].wait()
+    copies[0].wait()
     lax.fori_loop(0, total, invert, 0, unroll=8)
-    copies[3].wait()
+    copies[1].wait()
     me = lax.axis_index("ctx")
     for qb in range(blocks):
         row = order_ref[me * blocks + qb]
@@ -150,50 +167,54 @@
             return carry
 
         lax.fori_loop(0, slots, mark, 0, unroll=4)
-    copies[0].wait()
-    for j in range(rows // BLOCK_TOKENS):
-        for i in range(width // HEAD_SIZE):
-            turned = v_buf[tile(j), tile(i)].T
-            shard_ref[tile(rows // BLOCK_TOKENS + j), tile(i)] = turned
-            values_ref[tile(j), tile(i)] = turned
-    copies[1].wait()
-
-
-def tick_kernel(_shard, tick_ref):
-    tick_ref[0] = 0
-
-
-def own_kernel(blocks, kv_local, groups, flags_ref, q_ref, own_ref, qt_ref, ml_ref, acc_ref):
-    me = lax.axis_index("ctx")
-    total = flags_ref.shape[0] // blocks
+
+    def spread(i, carry):
+        gaps_ref[i] = jnp.full(gaps_ref.shape[1:], jnp.where(flags_ref[i] != 0, 0.0, FAR), jnp.float32)
+        return carry
+
+    lax.fori_loop(0, blocks * total, spread, 0, unroll=8)
+
+
+def own_kernel(blocks, kv_local, groups, gaps_ref, q_ref, own_ref, qt_ref, ml_ref, acc_ref):
     for qb in range(blocks):
         for h in range(kv_local * groups):
             qt_ref[qb, :, tile(h)] = q_ref[tile(qb), tile(h)].T
-        flags = [flags_ref[qb * total + me * blocks + j] for j in range(blocks)]
-        gaps = [0.0 if j == qb else jnp.where(flags[j] != 0, 0.0, FAR) for j in range(blocks)]
+        gaps, _ = gap_rows(gaps_ref, blocks, qb, 0)
+        gaps[qb] = 0.0
         attend(halves(own_ref), qb, qb, gaps, qb, kv_local, groups, qt_ref, ml_ref, acc_ref)
 
 
-def more_kernel(masks, pieces, blocks, kv_local, groups, flags_ref, qt_ref, ml_in, acc_in, *refs):
+def more_kernel(masks, pieces, blocks, kv_local, groups, gaps_ref, qt_ref, ml_in, acc_in, *refs):
     shards, (ml_ref, acc_ref) = split_shards(pieces, refs)
     ml_ref[...] = ml_in[...]
     acc_ref[...] = acc_in[...]
     attend_shards(
-        masks, blocks, 0, blocks, flags_ref, shards,
+        masks, blocks, 0, blocks, gaps_ref, shards,
         kv_local=kv_local, groups=groups, qt_ref=qt_ref, ml_ref=ml_ref, acc_ref=acc_ref,
     )
 
 
-def last_kernel(masks, pieces, blocks, part, step, cores, kv_local, groups, flags_ref, qt_ref, ml_in, acc_in, *refs):
-    shards, (out_ref, norm_ref, ml_ref, acc_ref) = split_shards(pieces, refs)
+def part_kernel(masks, pieces, blocks, part, step, cores, kv_local, groups, gaps_ref, qt_ref, ml_in, acc_in, *refs):
+    shards, (ml_ref, acc_ref) = split_shards(pieces, refs)
     to = lax.rem(lax.axis_index("tp") + step, cores)
     for j in range(part):
         ml_ref[j] = ml_in[to * part + j]
         acc_ref[j] = acc_in[to * part + j]
+    attend_shards(
+        masks, blocks, to * part, part, gaps_ref, shards,
+        kv_local=kv_local, groups=groups, qt_ref=qt_ref, ml_ref=ml_ref, acc_ref=acc_ref,
+    )
+
+
+def last_kernel(masks, pieces, blocks, part, step, cores, kv_local, groups, gaps_ref, qt_ref, ml_in, acc_in, *refs):
+    shards, (out_ref, norm_ref, ml_ref, acc_ref) = split_shards(pieces, refs)
+    to = lax.rem(lax.axis_index("tp") + step, cores)
+    first = 0 if step else to * part
+    for j in range(part):
+        ml_ref[j] = ml_in[first + j]
+        acc_ref[j] = acc_in[first + j]
     rest = dict(kv_local=kv_local, groups=groups, qt_ref=qt_ref, ml_ref=ml_ref, acc_ref=acc_ref)
-    attend_shards(masks[:-1], blocks, to * part, part, flags_ref, shards[:-1], **rest)
-    me = lax.axis_index("ctx")
-    total = flags_ref.shape[0] // blocks
+    attend_shards(masks[:-1], blocks, to * part, part, gaps_ref, shards[:-1], **rest)
     for j in range(part):
 
         def finish(h, peak, denominator, weighted):
@@ -202,15 +223,13 @@
             norm_ref[h : h + 1, tile(j)] = peak * LN2 + jnp.log(denominator)
 
         qb = to * part + j
-        mine = [flags_ref[qb * total + (me ^ masks[-1]) * blocks + b] for b in range(blocks)]
-        some = functools.reduce(jnp.bitwise_or, mine)
-
-        @pl.when(some != 0)
+        gaps, some = gap_rows(gaps_ref, blocks, qb, masks[-1])
+
+        @pl.when(some)
         def _():
-            gaps = [jnp.where(flag != 0, 0.0, FAR) for flag in mine]
             attend(shards[-1], qb, j, gaps, None, finish=finish, **rest)
 
-        @pl.when(some == 0)
+        @pl.when(jnp.logical_not(some))
         def _():
             for h in range(kv_local * groups):
                 finish(h, ml_ref[j, 0:1, tile(h)], ml_ref[j, 1:2, tile(h)], acc_ref[j, :, tile(h)])
@@ -247,7 +266,6 @@
     part = blocks // cores
 
     vmem = pl.BlockSpec(memory_space=pltpu.VMEM)
-    smem = pl.BlockSpec(memory_space=pltpu.SMEM)
     hbm = pl.BlockSpec(memory_space=pltpu.HBM)
     qt_shape = jax.ShapeDtypeStruct((blocks, HEAD_SIZE, width), jnp.bfloat16)
     ml_shape = jax.ShapeDtypeStruct((blocks, 2, width), jnp.float32)
@@ -262,30 +280,39 @@
             **options,
         )
 
+    def in_hbm(array):
+        return pltpu.with_memory_space_constraint(array, pltpu.HBM)
+
     def swap(array, distance):
         return lax.ppermute(array, "ctx", [(i, i ^ distance) for i in range(shards)])
 
     bits = [1 << i for i in range(shards.bit_length() - 1)]
     top = bits[-1]
-    shard, values, flags = call(
-        functools.partial(pack_kernel, blocks),
+    shard, values = call(
+        pack_kernel,
         "pack",
-        FULL_VMEM,
-        in_specs=[hbm] * 4,
-        out_specs=[vmem, vmem, smem],
+        in_specs=[hbm] * 2,
+        out_specs=[vmem] * 2,
         out_shape=[
             jax.ShapeDtypeStruct((2 * rows, kv_local * HEAD_SIZE), jnp.bfloat16),
             jax.ShapeDtypeStruct((rows, kv_local * HEAD_SIZE), jnp.bfloat16),
-            jax.ShapeDtypeStruct((blocks * block_order.shape[0] + 1,), jnp.int32),
         ],
+        scratch_shapes=[pltpu.VMEM(value_rows.shape, jnp.bfloat16), pltpu.SemaphoreType.DMA((2,))],
+    )(in_hbm(key_rows), in_hbm(value_rows))
+    gaps = call(
+        functools.partial(gaps_kernel, blocks),
+        "gaps",
+        in_specs=[hbm] * 2,
+        out_specs=vmem,
+        out_shape=jax.ShapeDtypeStruct((blocks * block_order.shape[0], 1, BLOCK_TOKENS), jnp.float32),
         scratch_shapes=[
-            pltpu.VMEM(value_rows.shape, jnp.bfloat16),
+            pltpu.SMEM((blocks * block_order.shape[0] + 1,), jnp.int32),
             pltpu.SMEM(block_order.shape, jnp.int32),
             pltpu.SMEM(live_blocks.shape, jnp.int32),
             pltpu.SMEM(block_order.shape, jnp.int32),
-            pltpu.SemaphoreType.DMA((4,)),
+            pltpu.SemaphoreType.DMA((2,)),
         ],
-    )(key_rows, value_rows, block_order, live_blocks)
+    )(in_hbm(block_order), in_hbm(live_blocks))
     got = {top: [swap(shard, top)]}
     for bit in reversed(bits[1:-1]):
         got[bit] = [swap(shard, bit)]
@@ -294,19 +321,19 @@
     qt, ml, acc = call(
         functools.partial(own_kernel, blocks, kv_local, groups),
         "own_shard",
-        in_specs=[smem] + [vmem] * 2,
+        in_specs=[vmem] * 3,
         out_specs=[vmem] * 3,
         out_shape=[qt_shape, ml_shape, acc_shape],
-    )(flags, queries, shard)
+    )(gaps, queries, shard)
 
     def more(masks, ml, acc):
         return call(
             functools.partial(more_kernel, masks, [len(got[m]) for m in masks], blocks, kv_local, groups),
             "more_shards",
-            in_specs=[smem] + [vmem] * (3 + sum(len(got[m]) for m in masks)),
+            in_specs=[vmem] * (4 + sum(len(got[m]) for m in masks)),
             out_specs=[vmem] * 2,
             out_shape=[ml_shape, acc_shape],
-        )(flags, qt, ml, acc, *[array for m in masks for array in got[m]])
+        )(gaps, qt, ml, acc, *[array for m in masks for array in got[m]])
 
     def last(masks, step, ml, acc):
         arrays = [array for m in masks for array in got[m]]
@@ -315,7 +342,7 @@
                 last_kernel, masks, [len(got[m]) for m in masks], blocks, part, step, cores, kv_local, groups
             ),
             "last_shards",
-            in_specs=[smem] + [vmem] * (3 + len(arrays)),
+            in_specs=[vmem] * (4 + len(arrays)),
             out_specs=[vmem, vmem],
             out_shape=[
                 jax.ShapeDtypeStruct((part * BLOCK_TOKENS, width), jnp.bfloat16),
@@ -325,7 +352,22 @@
                 pltpu.VMEM((part, *ml_shape.shape[1:]), jnp.float32),
                 pltpu.VMEM((part, *acc_shape.shape[1:]), jnp.float32),
             ],
-        )(flags, qt, ml, acc, *arrays)
+        )(gaps, qt, ml, acc, *arrays)
+
+    def more_of_part(masks, step, ml, acc):
+        arrays = [array for m in masks for array in got[m]]
+        return call(
+            functools.partial(
+                part_kernel, masks, [len(got[m]) for m in masks], blocks, part, step, cores, kv_local, groups
+            ),
+            "part_shards",
+            in_specs=[vmem] * (4 + len(arrays)),
+            out_specs=[vmem] * 2,
+            out_shape=[
+                jax.ShapeDtypeStruct((part, *ml_shape.shape[1:]), jnp.float32),
+                jax.ShapeDtypeStruct((part, *acc_shape.shape[1:]), jnp.float32),
+            ],
+        )(gaps, qt, ml, acc, *arrays)
 
     def after(arrays, *others):
         return [lax.optimization_barrier((array,) + others)[0] for array in arrays]
@@ -351,7 +393,10 @@
 
     outs, norms = [None] * cores, [None] * cores
     for step in range(cores - 1, -1, -1):
-        outs[step], norms[step] = last(final, step, ml, acc)
+        if step:
+            outs[step], norms[step] = last(final[1:], step, *more_of_part(final[:1], step, ml, acc))
+        else:
+            outs[step], norms[step] = last(final, step, ml, acc)
         if step:
             outs[step] = lax.ppermute(outs[step], "tp", [(i, (i + step) % cores) for i in range(cores)])
     return call(

time: 40.4 us -> 37.3 us (0.923)
  Pallas kernels: 21.7 us -> 18.9 us
  local copies, waits for them, and re-layouts: 2.83 us -> 1.22 us
  waiting for transfers between devices: 9.7 us -> 10.8 us
    pallas_call x2, Pallas kernels: 5.38 us -> 2.45 us  [last(): call(functools.partial(last_kernel, masks, [len(got[m]) for m in masks],...]
    unnamed x8 -> x2, local copies, waits for them, and re-layouts: 2.83 us -> 1.22 us
    pallas_call x1 -> x3, Pallas kernels: 1.95 us -> 3.08 us  [the longest x1 1.05 us: more_of_part(): call(functools.partial(part_kernel, masks, [len(got[m]) for m in masks],...]
    ppermute x8, waiting for transfers between devices: 9.7 us -> 10.7 us  [swap(): lax.ppermute(array, 'ctx', [(i, i ^ distance) for i in range(shards)])]
    pallas_call x1, Pallas kernels: 2.41 us -> 1.86 us  [body(): call(functools.partial(own_kernel, blocks, kv_local, groups), 'own_shard'...]
    pallas_call x3, Pallas kernels: 10.9 us -> 10.5 us  [more(): call(functools.partial(more_kernel, masks, [len(got[m]) for m in masks],...]
  transfers between devices with their start and end apart: 9 -> 9, of which waited for: 4 -> 4; matrix products, arithmetic and copies ran while one was open for 0% -> 0% of each run, Pallas kernels for 40% -> 45%
where the time goes in v1:
time: 37.3 us; the launch traced here: 36.9 us
  Pallas kernels  18.9 us (51%)
  waiting for transfers between devices  10.8 us (29%)
  starting transfers between devices  5.26 us (14%)
  local copies, waits for them, and re-layouts  1.22 us (3%)
  between operations  0.75 us (2%)
    ppermute x8, waiting for transfers between devices, swap(): lax.ppermute(array, 'ctx', [(i, i ^ distance) for i in range(shards)])  10.7 us
    pallas_call x3, Pallas kernels, more(): call(functools.partial(more_kernel, masks, [len(got[m]) for m in masks],...  10.5 us
    ppermute x1, starting transfers between devices, body(): lax.ppermute(outs[step], 'tp', [(i, (i + step) % cores) for i in range(co...  2.95 us
    pallas_call x2, Pallas kernels, last(): call(functools.partial(last_kernel, masks, [len(got[m]) for m in masks],...  2.45 us
    ppermute x8, starting transfers between devices, swap(): lax.ppermute(array, 'ctx', [(i, i ^ distance) for i in range(shards)])  2.31 us
    pallas_call x1, Pallas kernels, body(): call(functools.partial(own_kernel, blocks, kv_local, groups), 'own_shard'...  1.86 us
    unnamed x2, local copies, waits for them, and re-layouts  1.22 us
    pallas_call x1, Pallas kernels, more_of_part(): call(functools.partial(part_kernel, masks, [len(got[m]) for m in masks],...  1.05 us
  transfers between devices with their start and end apart: 9, of which 4 were waited for; matrix products, arithmetic and copies ran while one was open for 0% of the time, Pallas kernels for 45%

profile of v1, /device:TPU:29, one launch (start us, length us, event | category | flops | bytes accessed | tf_op | source)
XLA Modules:
  0.0 36.9 jit_solution(14596759292836937606)
XLA Ops:
  0.6 1.0 %pack.1 = (bf16[512,256]{1,0:T(8,128)(2,1)S(1)}, bf16[256,256]{1,0:T(8,128)(2,1)S(1)}) custom-call(bf16[256,256]{1,0:T(8,128)(2,1)} %k_hbm.1, bf16[256,256]{1,0:T(8,128)(2,1)} %v_hbm.1), custom_call_target="tpu_custom_call" | custom-call | flops 1024 | bytes 1024 | tf_op jit(solution)/shard_map/pack/pallas_call | solution.py:291
  1.6 0.1 collective-permute-start.3
  1.8 0.2 collective-permute-start.2
  2.0 0.2 collective-permute-start
  2.2 1.2 %collective-permute-start.1 = (bf16[256,256]{1,0:T(8,128)(2,1)S(1)}, bf16[256,256]{1,0:T(8,128)(2,1)S(1)}, u32[]{:S(2)}, u32[]{:S(2)}) collective-permute-start(bf16[256,256]{1,0:T(8,128)(2,1)S(1)} %get-tuple-element.29), channel_id=1, source_target_pairs={{0,2},{2,0},{4,6},{6,4},{8,10},{10,8},{12,14},{14,12},{1,3},{3,1},... | collective-permute-start | bytes 393224 | tf_op jit(solution)/shard_map/ppermute | solution.py:287
  3.4 1.0 %gaps.1.gaps_ref = f32[32,1,128]{2,1,0:T(1,128)S(1)} custom-call(s32[16]{0:T(128)} %order_hbm.1, s32[16,12]{1,0:T(8,128)} %live_hbm.1), custom_call_target="tpu_custom_call" | custom-call | flops 1024 | bytes 1024 | tf_op jit(solution)/shard_map/gaps/pallas_call | solution.py:302
  4.5 0.0 copy-start
  4.5 1.2 %copy-done = bf16[256,2048]{1,0:T(8,128)(2,1)S(1)} copy-done((bf16[256,2048]{1,0:T(8,128)(2,1)S(1)}, bf16[256,2048]{1,0:T(8,128)(2,1)}, u32[]{:S(2)}) %copy-start) | copy-done | bytes 1048600
  5.7 1.9 %own_shard.1 = (bf16[2,128,2048]{2,1,0:T(8,128)(2,1)S(1)}, f32[2,2,2048]{2,1,0:T(2,128)S(1)}, f32[2,128,2048]{2,1,0:T(8,128)S(1)}) custom-call(f32[32,1,128]{2,1,0:T(1,128)S(1)} %gaps.1.gaps_ref, bf16[256,2048]{1,0:T(8,128)(2,1)S(1)} %copy-done, bf16[512,256]{1,0:T(8,128)(2,1)S(1)} %get-tuple-element.25.own_ref), custom_call_target="tpu_custom_call" | custom-call | flops 1024 | bytes 1024 | tf_op jit(solution)/shard_map/own_shard/pallas_call | solution.py:321
  7.5 0.0 collective-permute-done.refs_0_
  7.6 1.2 %collective-permute-done.1.refs_1_ = bf16[256,256]{1,0:T(8,128)(2,1)S(1)} collective-permute-done((bf16[256,256]{1,0:T(8,128)(2,1)S(1)}, bf16[256,256]{1,0:T(8,128)(2,1)S(1)}, u32[]{:S(2)}, u32[]{:S(2)}) %collective-permute-start.1) | collective-permute-done | bytes 131104 | tf_op jit(solution)/shard_map/ppermute | solution.py:287
  8.8 2.2 %more_shards.3 = (f32[2,2,2048]{2,1,0:T(2,128)S(1)}, f32[2,128,2048]{2,1,0:T(8,128)S(1)}) custom-call(f32[32,1,128]{2,1,0:T(1,128)S(1)} %gaps.1.gaps_ref, bf16[2,128,2048]{2,1,0:T(8,128)(2,1)S(1)} %get-tuple-element.26.qt_ref, f32[2,2,2048]{2,1,0:T(2,128)S(1)} %get-tuple-element.27.ml_in, f32[2,128,2048]{2,1,0:T(8,128)S(1)} %get-tuple-element.28.acc_in, ...), custom_call_target="tpu_custom_call" | custom-call | flops 1024 | bytes 1024 | tf_op jit(solution)/shard_map/more_shards/pallas_call | solution.py:330
  11.0 5.4 %collective-permute-done.3.refs_1_ = bf16[512,256]{1,0:T(8,128)(2,1)S(1)} collective-permute-done((bf16[512,256]{1,0:T(8,128)(2,1)S(1)}, bf16[512,256]{1,0:T(8,128)(2,1)S(1)}, u32[]{:S(2)}, u32[]{:S(2)}) %collective-permute-start.3) | collective-permute-done | bytes 262176 | tf_op jit(solution)/shard_map/ppermute | solution.py:287
  16.3 0.0 collective-permute-done.2.refs_0_
  16.3 0.0 collective-permute-start.5
  16.4 0.2 collective-permute-start.4
  16.6 4.1 %more_shards.4 = (f32[2,2,2048]{2,1,0:T(2,128)S(1)}, f32[2,128,2048]{2,1,0:T(8,128)S(1)}) custom-call(f32[32,1,128]{2,1,0:T(1,128)S(1)} %gaps.1.gaps_ref, bf16[2,128,2048]{2,1,0:T(8,128)(2,1)S(1)} %get-tuple-element.26.qt_ref, f32[2,2,2048]{2,1,0:T(2,128)S(1)} %get-tuple-element.30.ml_in, f32[2,128,2048]{2,1,0:T(8,128)S(1)} %get-tuple-element.31.acc_in, ...), custom_call_target="tpu_custom_call" | custom-call | flops 1024 | bytes 1024 | tf_op jit(solution)/shard_map/more_shards/pallas_call | solution.py:330
  20.7 0.1 collective-permute-start.6
  20.8 2.9 %collective-permute-done.5.refs_1_ = bf16[512,256]{1,0:T(8,128)(2,1)S(1)} collective-permute-done((bf16[512,256]{1,0:T(8,128)(2,1)S(1)}, bf16[512,256]{1,0:T(8,128)(2,1)S(1)}, u32[]{:S(2)}, u32[]{:S(2)}) %collective-permute-start.5) | collective-permute-done | bytes 262176 | tf_op jit(solution)/shard_map/ppermute | solution.py:287
  23.7 0.2 collective-permute-start.7
  24.0 0.0 collective-permute-done.4.refs_0_
  24.0 4.1 %more_shards.5 = (f32[2,2,2048]{2,1,0:T(2,128)S(1)}, f32[2,128,2048]{2,1,0:T(8,128)S(1)}) custom-call(f32[32,1,128]{2,1,0:T(1,128)S(1)} %gaps.1.gaps_ref, bf16[2,128,2048]{2,1,0:T(8,128)(2,1)S(1)} %get-tuple-element.26.qt_ref, f32[2,2,2048]{2,1,0:T(2,128)S(1)} %get-tuple-element.35.ml_in, f32[2,128,2048]{2,1,0:T(8,128)S(1)} %get-tuple-element.36.acc_in, ...), custom_call_target="tpu_custom_call" | custom-call | flops 1024 | bytes 1024 | tf_op jit(solution)/shard_map/more_shards/pallas_call | solution.py:330
  28.1 1.2 %collective-permute-done.6.refs_0_ = bf16[512,256]{1,0:T(8,128)(2,1)S(1)} collective-permute-done((bf16[512,256]{1,0:T(8,128)(2,1)S(1)}, bf16[512,256]{1,0:T(8,128)(2,1)S(1)}, u32[]{:S(2)}, u32[]{:S(2)}) %collective-permute-start.6) | collective-permute-done | bytes 262176 | tf_op jit(solution)/shard_map/ppermute | solution.py:287
  29.4 1.1 %part_shards.1 = (f32[1,2,2048]{2,1,0:T(2,128)S(1)}, f32[1,128,2048]{2,1,0:T(8,128)S(1)}) custom-call(f32[32,1,128]{2,1,0:T(1,128)S(1)} %gaps.1.gaps_ref, bf16[2,128,2048]{2,1,0:T(8,128)(2,1)S(1)} %get-tuple-element.26.qt_ref, f32[2,2,2048]{2,1,0:T(2,128)S(1)} %get-tuple-element.37.ml_in, f32[2,128,2048]{2,1,0:T(8,128)S(1)} %get-tuple-element.38.acc_in, ...), custom_call_target="tpu_custom_call" | custom-call | flops 1024 | bytes 1024 | tf_op jit(solution)/shard_map/part_shards/pallas_call | solution.py:359
  30.4 0.0 collective-permute-done.7.refs_1_.refs_0_
  30.4 0.3 last_shards.3
  30.7 3.0 %collective-permute-start.8 = (bf16[128,2048]{1,0:T(8,128)(2,1)S(1)}, bf16[128,2048]{1,0:T(8,128)(2,1)S(1)}, u32[]{:S(2)}, u32[]{:S(2)}) collective-permute-start(bf16[128,2048]{1,0:T(8,128)(2,1)S(1)} %get-tuple-element.45), channel_id=1, source_target_pairs={{0,1},{1,0},{2,3},{3,2},{4,5},{5,4},{6,7},{7,6},{8,9},{9,8},{10,11... | collective-permute-start | bytes 1572872 | tf_op jit(solution)/shard_map/ppermute | solution.py:401
  33.7 2.1 %last_shards.2 = (bf16[128,2048]{1,0:T(8,128)(2,1)S(1)}, f32[16,128]{1,0:T(8,128)S(1)}) custom-call(f32[32,1,128]{2,1,0:T(1,128)S(1)} %gaps.1.gaps_ref, bf16[2,128,2048]{2,1,0:T(8,128)(2,1)S(1)} %get-tuple-element.26.qt_ref, f32[2,2,2048]{2,1,0:T(2,128)S(1)} %get-tuple-element.37.ml_in, f32[2,128,2048]{2,1,0:T(8,128)S(1)} %get-tuple-element.38.acc_in, ...), custom_call_target="tpu_custom_call" | custom-call | flops 1024 | bytes 1024 | tf_op jit(solution)/shard_map/last_shards/pallas_call | solution.py:340
  35.8 0.0 collective-permute-done.8.refs_1_
  35.9 1.0 %place.1 = (bf16[128,4096]{1,0:T(8,128)(2,1)}, f32[16,256]{1,0:T(8,128)}) custom-call(bf16[128,2048]{1,0:T(8,128)(2,1)S(1)} %get-tuple-element.42.refs_0_, bf16[128,2048]{1,0:T(8,128)(2,1)S(1)} %collective-permute-done.8.refs_1_, f32[16,128]{1,0:T(8,128)S(1)} %get-tuple-element.46.refs_2_, f32[16,128]{1,0:T(8,128)S(1)} %get-tuple-element.47.refs_3_), custom_call_target="tpu_custom_call" | custom-call | flops 1024 | bytes 1024 | tf_op jit(solution)/shard_map/place/pallas_call | solution.py:402
  (1 shorter events, 0.0 us)
Async XLA Ops:
  1.6 14.7 %collective-permute-start.3 = (bf16[512,256]{1,0:T(8,128)(2,1)S(1)}, bf16[512,256]{1,0:T(8,128)(2,1)S(1)}, u32[]{:S(2)}, u32[]{:S(2)}) collective-permute-start(bf16[512,256]{1,0:T(8,128)(2,1)S(1)} %get-tuple-element.25.own_ref), channel_id=1, source_target_pairs={{0,8},{2,10},{4,12},{6,14},{8,0},{10,2},{12,4},{14,6},{1,9},{3,11}... | collective-permute-start | bytes 786440 | tf_op jit(solution)/shard_map/ppermute | solution.py:287
  1.8 14.6 %collective-permute-start.2 = (bf16[512,256]{1,0:T(8,128)(2,1)S(1)}, bf16[512,256]{1,0:T(8,128)(2,1)S(1)}, u32[]{:S(2)}, u32[]{:S(2)}) collective-permute-start(bf16[512,256]{1,0:T(8,128)(2,1)S(1)} %get-tuple-element.25.own_ref), channel_id=1, source_target_pairs={{0,4},{2,6},{4,0},{6,2},{8,12},{10,14},{12,8},{14,10},{1,5},{3,7},... | collective-permute-start | bytes 786440 | tf_op jit(solution)/shard_map/ppermute | solution.py:287
  2.0 5.6 %collective-permute-start = (bf16[256,256]{1,0:T(8,128)(2,1)}, bf16[256,256]{1,0:T(8,128)(2,1)S(1)}, u32[]{:S(2)}, u32[]{:S(2)}) collective-permute-start(bf16[256,256]{1,0:T(8,128)(2,1)} %k_hbm.1), channel_id=1, source_target_pairs={{0,2},{2,0},{4,6},{6,4},{8,10},{10,8},{12,14},{14,12},{1,3},{3,1},... | collective-permute-start | bytes 393224 | tf_op jit(solution)/shard_map/ppermute | solution.py:287
  2.2 6.6 %collective-permute-start.1 = (bf16[256,256]{1,0:T(8,128)(2,1)S(1)}, bf16[256,256]{1,0:T(8,128)(2,1)S(1)}, u32[]{:S(2)}, u32[]{:S(2)}) collective-permute-start(bf16[256,256]{1,0:T(8,128)(2,1)S(1)} %get-tuple-element.29), channel_id=1, source_target_pairs={{0,2},{2,0},{4,6},{6,4},{8,10},{10,8},{12,14},{14,12},{1,3},{3,1},... | collective-permute-start | bytes 393224 | tf_op jit(solution)/shard_map/ppermute | solution.py:287
  4.5 1.2 %copy-start = (bf16[256,2048]{1,0:T(8,128)(2,1)S(1)}, bf16[256,2048]{1,0:T(8,128)(2,1)}, u32[]{:S(2)}) copy-start(bf16[256,2048]{1,0:T(8,128)(2,1)} %q_ref.1) | copy-start | bytes 3145732
  16.3 7.4 %collective-permute-start.5 = (bf16[512,256]{1,0:T(8,128)(2,1)S(1)}, bf16[512,256]{1,0:T(8,128)(2,1)S(1)}, u32[]{:S(2)}, u32[]{:S(2)}) collective-permute-start(bf16[512,256]{1,0:T(8,128)(2,1)S(1)} %collective-permute-done.3.refs_1_), channel_id=1, source_target_pairs={{0,4},{2,6},{4,0},{6,2},{8,12},{10,14},{12,8},{14,10},{1,5},{3,7},... | collective-permute-start | bytes 786440 | tf_op jit(solution)/shard_map/ppermute | solution.py:287
  16.4 7.6 %collective-permute-start.4 = (bf16[512,256]{1,0:T(8,128)(2,1)S(1)}, bf16[512,256]{1,0:T(8,128)(2,1)S(1)}, u32[]{:S(2)}, u32[]{:S(2)}) collective-permute-start(bf16[512,256]{1,0:T(8,128)(2,1)S(1)} %collective-permute-done.3.refs_1_), channel_id=1, source_target_pairs={{0,2},{2,0},{4,6},{6,4},{8,10},{10,8},{12,14},{14,12},{1,3},{3,1},... | collective-permute-start | bytes 786440 | tf_op jit(solution)/shard_map/ppermute | solution.py:287
  20.7 8.6 %collective-permute-start.6 = (bf16[512,256]{1,0:T(8,128)(2,1)S(1)}, bf16[512,256]{1,0:T(8,128)(2,1)S(1)}, u32[]{:S(2)}, u32[]{:S(2)}) collective-permute-start(bf16[512,256]{1,0:T(8,128)(2,1)S(1)} %pad_maximum_fusion), channel_id=1, source_target_pairs={{0,4},{2,6},{4,0},{6,2},{8,12},{10,14},{12,8},{14,10},{1,5},{3,7},... | collective-permute-start | bytes 786440 | tf_op jit(solution)/shard_map/ppermute | solution.py:287
  23.7 6.7 %collective-permute-start.7 = (bf16[512,256]{1,0:T(8,128)(2,1)S(1)}, bf16[512,256]{1,0:T(8,128)(2,1)S(1)}, u32[]{:S(2)}, u32[]{:S(2)}) collective-permute-start(bf16[512,256]{1,0:T(8,128)(2,1)S(1)} %collective-permute-done.5.refs_1_), channel_id=1, source_target_pairs={{0,2},{2,0},{4,6},{6,4},{8,10},{10,8},{12,14},{14,12},{1,3},{3,1},... | collective-permute-start | bytes 786440 | tf_op jit(solution)/shard_map/ppermute | solution.py:287
  30.7 5.1 %collective-permute-start.8 = (bf16[128,2048]{1,0:T(8,128)(2,1)S(1)}, bf16[128,2048]{1,0:T(8,128)(2,1)S(1)}, u32[]{:S(2)}, u32[]{:S(2)}) collective-permute-start(bf16[128,2048]{1,0:T(8,128)(2,1)S(1)} %get-tuple-element.45), channel_id=1, source_target_pairs={{0,1},{1,0},{2,3},{3,2},{4,5},{5,4},{6,7},{7,6},{8,9},{9,8},{10,11... | collective-permute-start | bytes 1572872 | tf_op jit(solution)/shard_map/ppermute | solution.py:401
